TPU v7x, 32 devices: a whole 2x2x4 slice. The times are simulated.
32 devices in a mesh: replica: 8 (over y, x, core), shard: 4 (over z).
Axes of the slice: x: 2, y: 2, z: 4, core: 2. Of those that a mesh axis runs over, the one named last changes fastest.
Arguments:
- inputs: bfloat16 [8, 1024, 1024], P('replica', 'shard'), may hold values from -6 to 6
- out_grad: bfloat16 [8, 1024, 1024], P('replica', 'shard'), may hold values from -6 to 6
- segment_ids: int32 [8, 1024], P('replica'), may hold values from 0 to 2, never falling along the last dimension, each value on 1 to 512 neighbouring positions
- ln_gain_attn: bfloat16 [1024], P('shard'), may hold values from 0.5 to 1.5
- ln_bias_attn: bfloat16 [1024], P('shard'), may hold values from -3 to 3
- ln_gain_mlp: bfloat16 [1024], P('shard'), may hold values from 0.5 to 1.5
- ln_bias_mlp: bfloat16 [1024], P('shard'), may hold values from -3 to 3
- qkv_weight: bfloat16 [1024, 3072], P('shard'), may hold values from -0.1875 to 0.1875
- qkv_bias: bfloat16 [3072], P('shard'), may hold values from -3 to 3
- out_weight: bfloat16 [1024, 1024], P('shard'), may hold values from -0.75 to 0.75
- up_weight: bfloat16 [1024, 4096], P('shard'), may hold values from -0.1875 to 0.1875
- up_bias: bfloat16 [4096], P('shard'), may hold values from -3 to 3
- down_weight: bfloat16 [4096, 1024], P('shard'), may hold values from -0.09375 to 0.09375
- output_bias: bfloat16 [1024], P('shard'), may hold values from -3 to 3
Outputs:
- outputs: bfloat16 [8, 1024, 1024], P('replica', 'shard')
- in_grad: bfloat16 [8, 1024, 1024], P('replica', 'shard')
- grad_ln_gain_attn: float32 [1024], P('shard')
- grad_ln_bias_attn: float32 [1024], P('shard')
- grad_ln_gain_mlp: float32 [1024], P('shard')
- grad_ln_bias_mlp: float32 [1024], P('shard')
- grad_qkv_weight: float32 [1024, 3072], P('shard')
- grad_qkv_bias: float32 [3072], P('shard')
- grad_out_weight: float32 [1024, 1024], P('shard')
- grad_up_weight: float32 [1024, 4096], P('shard')
- grad_up_bias: float32 [4096], P('shard')
- grad_down_weight: float32 [4096, 1024], P('shard')
- grad_output_bias: float32 [1024], P('shard')
Inputs may be any that keep to these rules, and one draw needn't show every extreme that they name: `segment_ids`: in every sequence the document numbers never fall and run through 0 to 2; every document has 1 to 512 tokens, one exactly 512.
All inputs are finite; a program needn't handle non-finite values.
Results may differ from a plain program's by a relative error of at most 0.012.
Values may be sent and summed in bfloat16 or wider, within the bound.
A program may use at most 256 MiB of HBM per device.

v0:
```python
from functools import partial
import jax
import jax.numpy as jnp
from jax import lax
from jax.sharding import PartitionSpec as P

D = 1024
FF = 4096
HEADS = 16
HEAD = 64
ROT = 16
DOCS = 3


def layer_norm(values, gain, shift):
    centered = values - jnp.mean(values, axis=-1, keepdims=True)
    variance = jnp.mean(centered * centered, axis=-1, keepdims=True)
    return centered * lax.rsqrt(variance + 1e-05) * gain + shift


def exact_gelu(values):
    return jax.nn.gelu(values, approximate=False)


def doc_positions(segment_row):
    documents = jnp.arange(DOCS, dtype=jnp.int32)
    member = (segment_row[:, None] == documents[None, :]).astype(jnp.int32)
    counts = jnp.sum(member, axis=0)
    starts = jnp.cumsum(counts) - counts
    doc_start = jnp.sum(member * starts[None, :], axis=1)
    return jnp.arange(segment_row.shape[0], dtype=jnp.int32) - doc_start


def rotate(features, positions):
    half_rot = ROT // 2
    inv_freq = 1.0 / 10000.0 ** (jnp.arange(half_rot, dtype=jnp.float32) * 2.0 / ROT)
    angles = positions.astype(jnp.float32)[..., None] * inv_freq
    cosine = jnp.cos(angles)[..., None, :]
    sine_part = jnp.sin(angles)[..., None, :]
    front_half = features[..., :half_rot]
    back_half = features[..., half_rot:ROT]
    return jnp.concatenate(
        [
            front_half * cosine - back_half * sine_part,
            back_half * cosine + front_half * sine_part,
            features[..., ROT:],
        ],
        axis=-1,
    )


def masked_scores(queries, key_rows, segment_row, first_row):
    local_len = queries.shape[0]
    query_at = first_row + jnp.arange(local_len, dtype=jnp.int32)
    key_at = jnp.arange(key_rows.shape[0], dtype=jnp.int32)
    query_doc = lax.dynamic_slice_in_dim(segment_row, first_row, local_len, 0)
    allowed = (key_at[None, :] <= query_at[:, None]) & (segment_row[None, :] == query_doc[:, None])
    score_scale = queries.shape[-1] ** (-0.5)
    scores = (
        jnp.einsum("qhd,khd->hqk", queries, key_rows, preferred_element_type=jnp.float32)
        * score_scale
    )
    return jnp.where(allowed[None], scores, -1e30)


def attend_forward(first_row, element):
    queries, key_rows, value_rows, segment_row = element
    scores = masked_scores(queries, key_rows, segment_row, first_row)
    row_max = jnp.max(scores, axis=-1, keepdims=True)
    shifted_exp = jnp.exp(scores - row_max)
    row_sum = jnp.sum(shifted_exp, axis=-1, keepdims=True)
    probs = (shifted_exp / row_sum).astype(jnp.bfloat16)
    context = jnp.einsum("hqk,khd->qhd", probs, value_rows, preferred_element_type=jnp.float32)
    return (context.astype(jnp.bfloat16), row_max + jnp.log(row_sum))


def attend_backward(first_row, element):
    queries, key_rows, value_rows, segment_row, log_norm, grad_context = element
    scores = masked_scores(queries, key_rows, segment_row, first_row)
    weights = jnp.exp(scores - log_norm)
    grad_probs = jnp.einsum(
        "qhd,khd->hqk", grad_context, value_rows, preferred_element_type=jnp.float32
    )
    row_inner = jnp.sum(weights * grad_probs, axis=-1, keepdims=True)
    grad_scores = (weights * (grad_probs - row_inner)).astype(jnp.bfloat16)
    score_scale = queries.shape[-1] ** (-0.5)
    grad_query = (
        jnp.einsum("hqk,khd->qhd", grad_scores, key_rows, preferred_element_type=jnp.float32)
        * score_scale
    )
    grad_key = (
        jnp.einsum("hqk,qhd->khd", grad_scores, queries, preferred_element_type=jnp.float32)
        * score_scale
    )
    grad_value = jnp.einsum(
        "hqk,qhd->khd",
        weights.astype(jnp.bfloat16),
        grad_context,
        preferred_element_type=jnp.float32,
    )
    return (grad_query, grad_key, grad_value)


def shards(
    inputs,
    out_grad,
    segment_ids,
    ln_gain_attn,
    ln_bias_attn,
    ln_gain_mlp,
    ln_bias_mlp,
    qkv_weight,
    qkv_bias,
    out_weight,
    up_weight,
    up_bias,
    down_weight,
    output_bias,
):
    seq_count, local_len, model_width = inputs.shape
    token_count = seq_count * local_len
    first_row = lax.axis_index("shard") * local_len
    group_ratio = FF // D
    flat_in = inputs.reshape(token_count, model_width).astype(jnp.float32)
    gain_attn, shift_attn, gain_mlp, shift_mlp, qkv_shift, up_shift, out_shift = (
        lax.all_gather(ln_gain_attn, "shard", axis=0, tiled=True),
        lax.all_gather(ln_bias_attn, "shard", axis=0, tiled=True),
        lax.all_gather(ln_gain_mlp, "shard", axis=0, tiled=True),
        lax.all_gather(ln_bias_mlp, "shard", axis=0, tiled=True),
        lax.all_gather(qkv_bias, "shard", axis=0, tiled=True),
        lax.all_gather(up_bias, "shard", axis=0, tiled=True),
        lax.all_gather(output_bias, "shard", axis=0, tiled=True),
    )
    attn_float, attn_pullback = jax.vjp(
        layer_norm, flat_in, gain_attn.astype(jnp.float32), shift_attn.astype(jnp.float32)
    )
    mlp_float, mlp_pullback = jax.vjp(
        layer_norm, flat_in, gain_mlp.astype(jnp.float32), shift_mlp.astype(jnp.float32)
    )
    attn_normed = attn_float.astype(jnp.bfloat16)
    mlp_normed = mlp_float.astype(jnp.bfloat16)
    pieces = (
        lax.all_gather(qkv_weight, "shard", axis=0, tiled=True),
        lax.all_gather(up_weight, "shard", axis=0, tiled=True),
    )
    qkv_sum = jnp.dot(attn_normed, pieces[0], preferred_element_type=jnp.float32)
    up_sum = jnp.dot(mlp_normed, pieces[1], preferred_element_type=jnp.float32)
    qkv_parts = (qkv_sum + qkv_shift.astype(jnp.float32)).reshape(
        seq_count, local_len, 3, HEADS, HEAD
    )
    all_positions = jax.vmap(doc_positions)(segment_ids)
    own_positions = lax.dynamic_slice_in_dim(all_positions, first_row, local_len, 1)

    def rotate_pair(query_part, key_part):
        return (rotate(query_part, own_positions), rotate(key_part, own_positions))

    (query_rot, key_rot), rotate_pullback = jax.vjp(
        rotate_pair, qkv_parts[:, :, 0], qkv_parts[:, :, 1]
    )
    query_low = query_rot.astype(jnp.bfloat16)
    key_low = key_rot.astype(jnp.bfloat16)
    value_low = qkv_parts[:, :, 2].astype(jnp.bfloat16)
    key_all, value_all = (
        lax.all_gather(key_low, "shard", axis=1, tiled=True),
        lax.all_gather(value_low, "shard", axis=1, tiled=True),
    )
    context_seq, log_norms = lax.map(
        partial(attend_forward, first_row), (query_low, key_all, value_all, segment_ids)
    )
    context_low = context_seq.reshape(token_count, model_width)
    hidden_act, gelu_pullback = jax.vjp(exact_gelu, up_sum + up_shift.astype(jnp.float32))
    hidden_low = hidden_act.astype(jnp.bfloat16)
    down_grouped = down_weight.reshape(-1, group_ratio * model_width)
    pieces = (
        lax.all_gather(out_weight, "shard", axis=0, tiled=True),
        lax.all_gather(down_grouped, "shard", axis=0, tiled=True),
    )
    piece_rows = pieces[0].shape[0]
    down_rows = pieces[1].reshape(piece_rows * group_ratio, model_width)
    mixed = jnp.dot(context_low, pieces[0], preferred_element_type=jnp.float32) + jnp.dot(
        hidden_low, down_rows, preferred_element_type=jnp.float32
    )
    result = flat_in + mixed + out_shift.astype(jnp.float32)
    outputs = result.astype(jnp.bfloat16).reshape(seq_count, local_len, model_width)
    grad_low = out_grad.reshape(token_count, model_width)
    grad_float = grad_low.astype(jnp.float32)
    grad_out_shift = jnp.sum(grad_float, axis=0)
    grad_out_weight = jnp.einsum(
        "tk,tn->kn", context_low, grad_low, preferred_element_type=jnp.float32
    )
    grad_down_weight = jnp.einsum(
        "tk,tn->kn", hidden_low, grad_low, preferred_element_type=jnp.float32
    )
    out_shares = (
        lax.psum_scatter(grad_out_weight, "shard", scatter_dimension=0, tiled=True),
        lax.psum_scatter(grad_down_weight, "shard", scatter_dimension=0, tiled=True),
        lax.psum_scatter(grad_out_shift, "shard", scatter_dimension=0, tiled=True),
    )
    out_totals = lax.psum((out_shares[0], out_shares[1], out_shares[2]), "replica")
    pieces = (
        lax.all_gather(out_weight, "shard", axis=0, tiled=True),
        lax.all_gather(down_grouped, "shard", axis=0, tiled=True),
    )
    piece_rows = pieces[0].shape[0]
    down_rows = pieces[1].reshape(piece_rows * group_ratio, model_width)
    context_part = jnp.einsum("tn,kn->tk", grad_low, pieces[0], preferred_element_type=jnp.float32)
    hidden_part = jnp.einsum("tn,kn->tk", grad_low, down_rows, preferred_element_type=jnp.float32)
    context_grad_low = context_part.astype(jnp.bfloat16).reshape(seq_count, local_len, HEADS, HEAD)
    hidden_grad_low = gelu_pullback(hidden_part)[0].astype(jnp.bfloat16)
    key_back, value_back = (key_all, value_all)
    grad_query, key_part, value_part = lax.map(
        partial(attend_backward, first_row),
        (query_low, key_back, value_back, segment_ids, log_norms, context_grad_low),
    )
    grad_key, grad_value = (
        lax.psum_scatter(key_part, "shard", scatter_dimension=1, tiled=True),
        lax.psum_scatter(value_part, "shard", scatter_dimension=1, tiled=True),
    )
    query_pre, key_pre = rotate_pullback((grad_query, grad_key))
    grad_qkv = (
        jnp.stack([query_pre, key_pre, grad_value], axis=2)
        .reshape(token_count, 3 * model_width)
        .astype(jnp.bfloat16)
    )
    grad_qkv_shift = jnp.sum(grad_qkv.astype(jnp.float32), axis=0)
    grad_up_shift = jnp.sum(hidden_grad_low.astype(jnp.float32), axis=0)
    grad_qkv_weight = jnp.einsum(
        "tk,tn->kn", attn_normed, grad_qkv, preferred_element_type=jnp.float32
    )
    grad_up_weight = jnp.einsum(
        "tk,tn->kn", mlp_normed, hidden_grad_low, preferred_element_type=jnp.float32
    )
    pieces = (
        lax.all_gather(qkv_weight, "shard", axis=0, tiled=True),
        lax.all_gather(up_weight, "shard", axis=0, tiled=True),
    )
    attn_part = jnp.einsum("tn,kn->tk", grad_qkv, pieces[0], preferred_element_type=jnp.float32)
    mlp_part = jnp.einsum(
        "tn,kn->tk", hidden_grad_low, pieces[1], preferred_element_type=jnp.float32
    )
    attn_input, grad_gain_attn, grad_shift_attn = attn_pullback(attn_part)
    mlp_input, grad_gain_mlp, grad_shift_mlp = mlp_pullback(mlp_part)
    in_grad = (
        (grad_float + attn_input + mlp_input)
        .astype(jnp.bfloat16)
        .reshape(seq_count, local_len, model_width)
    )
    in_shares = (
        lax.psum_scatter(grad_gain_attn, "shard", scatter_dimension=0, tiled=True),
        lax.psum_scatter(grad_shift_attn, "shard", scatter_dimension=0, tiled=True),
        lax.psum_scatter(grad_gain_mlp, "shard", scatter_dimension=0, tiled=True),
        lax.psum_scatter(grad_shift_mlp, "shard", scatter_dimension=0, tiled=True),
        lax.psum_scatter(grad_qkv_weight, "shard", scatter_dimension=0, tiled=True),
        lax.psum_scatter(grad_qkv_shift, "shard", scatter_dimension=0, tiled=True),
        lax.psum_scatter(grad_up_weight, "shard", scatter_dimension=0, tiled=True),
        lax.psum_scatter(grad_up_shift, "shard", scatter_dimension=0, tiled=True),
    )
    in_totals = lax.psum(
        (
            in_shares[0],
            in_shares[1],
            in_shares[2],
            in_shares[3],
            in_shares[4],
            in_shares[5],
            in_shares[6],
            in_shares[7],
        ),
        "replica",
    )
    return (
        outputs,
        in_grad,
        in_totals[0],
        in_totals[1],
        in_totals[2],
        in_totals[3],
        in_totals[4],
        in_totals[5],
        out_totals[0],
        in_totals[6],
        in_totals[7],
        out_totals[1],
        out_totals[2],
    )


def solution(mesh):
    placed = (
        P("replica", "shard", None),
        P("replica", "shard", None),
        P("replica", None),
        P("shard"),
        P("shard"),
        P("shard"),
        P("shard"),
        P("shard", None),
        P("shard"),
        P("shard", None),
        P("shard", None),
        P("shard"),
        P("shard", None),
        P("shard"),
    )
    return jax.shard_map(
        shards,
        mesh=mesh,
        in_specs=placed,
        out_specs=(
            P("replica", "shard", None),
            P("replica", "shard", None),
            P("shard"),
            P("shard"),
            P("shard"),
            P("shard"),
            P("shard", None),
            P("shard"),
            P("shard", None),
            P("shard", None),
            P("shard"),
            P("shard", None),
            P("shard"),
        ),
        check_vma=False,
    )
```

profile of v0, /device:TPU:0, one launch (start us, length us, event | category | flops | bytes accessed | tf_op | source)
XLA Modules:
  0.0 1781.5 jit_solution(8662586912904173164)
XLA Ops:
  9.4 14.7 all-gather.3
  24.8 11.0 all-gather.2
  36.4 8.2 all-gather.1
  50.4 77.4 %all-gather.14.cloned.1.call-done = bf16[1024,3072]{1,0:T(8,128)(2,1)} async-done(((bf16[256,3072]{1,0:T(8,128)(2,1)}), bf16[1024,3072]{1,0:T(8,128)(2,1)}) %all-gather.14.cloned.1.call-update) | async-done | bytes 6291472 | tf_op jit(solution)/shard_map/all_gather | solution.py:143
  146.5 27.0 %all-gather.18.cloned.1.call-done = bf16[1024,1024]{1,0:T(8,128)(2,1)} async-done(((bf16[256,1024]{1,0:T(8,128)(2,1)}), bf16[1024,1024]{1,0:T(8,128)(2,1)}) %all-gather.18.cloned.1.call-update) | async-done | bytes 2097168 | tf_op jit(solution)/shard_map/all_gather | solution.py:175
  177.3 43.3 %all-gather.16.cloned.1.call-done = bf16[1,1024,16,64]{1,3,2,0:T(8,128)(2,1)} async-done(((bf16[1,256,16,64]{1,3,2,0:T(8,128)(2,1)}), bf16[1,1024,16,64]{1,3,2,0:T(8,128)(2,1)}) %all-gather.16.cloned.1.call-update) | async-done | bytes 2097168 | tf_op jit(solution)/shard_map/all_gather | solution.py:164
  231.9 35.2 %all-gather.24.cloned.1.call-done = bf16[1,1024,1,16,64]{1,4,3,2,0:T(8,128)(2,1)} async-done(((bf16[1,256,1,16,64]{1,4,3,2,0:T(8,128)(2,1)}), bf16[1,1024,1,16,64]{1,4,3,2,0:T(8,128)(2,1)}) %all-gather.24.cloned.1.call-update) | async-done | bytes 2097168 | tf_op jit(solution)/shard_map/all_gather | solution.py:165
  267.2 15.4 multiply_reduce_fusion
  284.8 7.8 multiply_convert_fusion
  300.1 9.4 fusion.12
  311.2 7.5 fusion.41
  322.9 14.4 all_gather.53
  337.3 8.8 all-gather.5
  346.1 11.3 all-gather.4
  357.5 59.8 %all-gather.22.cloned.1.call-done = bf16[1024,4096]{1,0:T(8,128)(2,1)} async-done(((bf16[256,4096]{1,0:T(8,128)(2,1)}), bf16[1024,4096]{1,0:T(8,128)(2,1)}) %all-gather.22.cloned.1.call-update) | async-done | bytes 8388624 | tf_op jit(solution)/shard_map/all_gather | solution.py:176
  417.3 14.2 reshape.567
  431.5 135.1 %all-gather.20.cloned.1.call-done = bf16[1024,4096]{1,0:T(8,128)(2,1)} async-done(((bf16[256,4096]{1,0:T(8,128)(2,1)}), bf16[1024,4096]{1,0:T(8,128)(2,1)}) %all-gather.20.cloned.1.call-update) | async-done | bytes 8388624 | tf_op jit(solution)/shard_map/all_gather | solution.py:144
  566.6 15.8 multiply_convert_fusion.1
  582.5 7.7 convert_reduce_fusion
  591.5 8.3 fusion.92
  600.0 8.1 fusion.66
  616.7 27.2 %reduce-scatter.7.cloned.1.call-done = f32[1,256,16,64]{1,3,2,0:T(8,128)} async-done(((f32[1,1024,16,64]{1,3,2,0:T(8,128)}), f32[1,256,16,64]{1,3,2,0:T(8,128)}) %reduce-scatter.7.cloned.1.call-update) | async-done | bytes 1048592 | tf_op jit(solution)/shard_map/reduce_scatter | solution.py:216
  647.3 76.4 %reduce-scatter.9.cloned.1.call-done = f32[1,256,16,64]{1,3,2,0:T(8,128)} async-done(((f32[1,1024,16,64]{1,3,2,0:T(8,128)}), f32[1,256,16,64]{1,3,2,0:T(8,128)}) %reduce-scatter.9.cloned.1.call-update) | async-done | bytes 1048592 | tf_op jit(solution)/shard_map/reduce_scatter | solution.py:217
  725.5 7.7 fusion.62
  733.2 70.0 %reduce-scatter.13.cloned.1.call-done = f32[256,1024]{1,0:T(8,128)} async-done(((f32[1024,1024]{1,0:T(8,128)}), f32[256,1024]{1,0:T(8,128)}) %reduce-scatter.13.cloned.1.call-update) | async-done | bytes 1048592 | tf_op jit(solution)/shard_map/reduce_scatter | solution.py:195
  803.2 283.2 %reduce-scatter.15.cloned.1.call-done = f32[256,4096]{1,0:T(8,128)} async-done(((f32[1024,4096]{1,0:T(8,128)}), f32[256,4096]{1,0:T(8,128)}) %reduce-scatter.15.cloned.1.call-update) | async-done | bytes 4194320 | tf_op jit(solution)/shard_map/reduce_scatter | solution.py:255
  1086.4 283.4 %reduce-scatter.17.cloned.1.call-done = f32[1024,1024]{1,0:T(8,128)} async-done(((f32[4096,1024]{1,0:T(8,128)}), f32[1024,1024]{1,0:T(8,128)}) %reduce-scatter.17.cloned.1.call-update) | async-done | bytes 4194320 | tf_op jit(solution)/shard_map/reduce_scatter | solution.py:196
  1369.8 214.9 %reduce-scatter.11.cloned.1.call-done = f32[256,3072]{1,0:T(8,128)} async-done(((f32[1024,3072]{1,0:T(8,128)}), f32[256,3072]{1,0:T(8,128)}) %reduce-scatter.11.cloned.1.call-update) | async-done | bytes 3145744 | tf_op jit(solution)/shard_map/reduce_scatter | solution.py:253
  1585.4 10.9 all-gather.6
  1622.1 16.8 all-reduce.15
  1639.3 23.6 %all-reduce.13 = (f32[256]{0:T(256)}, f32[256]{0:T(256)}, f32[256]{0:T(256)}, f32[256]{0:T(256)}, f32[768]{0:T(1024)}, /*index=5*/f32[1024]{0:T(1024)}, f32[256]{0:T(256)}) all-reduce(f32[256]{0:T(256)S(1)} %dynamic-slice.3, f32[256]{0:T(256)S(1)} %dynamic-slice.5, ...), channel_id=1, replica_groups=mesh['replica'=8,'shard'=4] {'replica'}, use_global_device_ids=true, to_apply=%region_16.17 | all-reduce | flops 3072 | bytes 24576 | tf_op jit(solution)/shard_map/psum | solution.py:258
  1662.9 101.0 %all-reduce.18.cloned.1.call-done = (f32[256,3072]{1,0:T(8,128)}, f32[256,1024]{1,0:T(8,128)}, f32[256,4096]{1,0:T(8,128)}, f32[1024,1024]{1,0:T(8,128)}) async-done(((f32[256,3072]{1,0:T(8,128)}, f32[256,1024]{1,0:T(8,128)}, f32[256,4096]{1,0:T(8,128)}, f32[1024,1024]{1,0:T(8,128)}), (f32[256,3072]{1,0:T(8,128)}, f32[256,1024]{1,0:T(8,128)}, f32[256,4096]{1,0:T(8,128)}, ...) | async-done | bytes 12582928 | tf_op jit(solution)/shard_map/psum | solution.py:258
  (198 shorter events, 109.2 us)
Async XLA Ops:
  7.2 120.6 %all-gather.14.cloned.1.call-start = ((), (), s32[]{:S(2)}) async-start(), calls=%async_computation.6 | async-start | bytes 7864320 | tf_op jit(solution)/shard_map/all_gather | solution.py:143
  7.9 165.6 %all-gather.18.cloned.1.call-start = ((), (), s32[]{:S(2)}) async-start(), calls=%async_computation.8 | async-start | bytes 2621440 | tf_op jit(solution)/shard_map/all_gather | solution.py:175
  8.7 212.0 %all-gather.16.cloned.1.call-start = ((), (), s32[]{:S(2)}) async-start(), calls=%async_computation.7 | async-start | bytes 2621440 | tf_op jit(solution)/shard_map/all_gather | solution.py:164
  50.3 84.1 %copy-start.37 = (f32[256]{0:T(256)}, f32[256]{0:T(256)S(1)}, u32[]{:S(2)}) copy-start(f32[256]{0:T(256)S(1)} %fusion.53) | copy-start | bytes 3076
  50.3 84.1 %copy-start.32 = (f32[256]{0:T(256)}, f32[256]{0:T(256)S(1)}, u32[]{:S(2)}) copy-start(f32[256]{0:T(256)S(1)} %fusion.89) | copy-start | bytes 3076
  50.4 86.7 %copy-start.28 = (f32[256,8]{0,1:T(8,128)}, f32[256,8]{0,1:T(8,128)S(1)}, u32[]{:S(2)}) copy-start(f32[256,8]{0,1:T(8,128)S(1)} %get-tuple-element.122) | copy-start | bytes 24580
  50.4 86.7 %copy-start.29 = (f32[256,8]{0,1:T(8,128)}, f32[256,8]{0,1:T(8,128)S(1)}, u32[]{:S(2)}) copy-start(f32[256,8]{0,1:T(8,128)S(1)} %get-tuple-element.123) | copy-start | bytes 24580
  139.6 127.6 %all-gather.24.cloned.1.call-start = ((), (), s32[]{:S(2)}) async-start(), calls=%async_computation.17 | async-start | bytes 2621440 | tf_op jit(solution)/shard_map/all_gather | solution.py:165
  140.5 33.0 %copy-start.5 = (bf16[1,256,1024]{2,1,0:T(8,128)(2,1)S(1)}, bf16[1,256,1024]{2,1,0:T(8,128)(2,1)}, u32[]{:S(2)}) copy-start(bf16[1,256,1024]{2,1,0:T(8,128)(2,1)} %param.15) | copy-start | bytes 1572868
  140.5 276.7 %all-gather.22.cloned.1.call-start = ((), (), s32[]{:S(2)}) async-start(), calls=%async_computation.10 | async-start | bytes 10485760 | tf_op jit(solution)/shard_map/all_gather | solution.py:176
  145.0 75.6 %copy-start.21 = (bf16[256,16,8]{0,2,1:T(8,128)(2,1)S(1)}, bf16[256,16,8]{0,2,1:T(8,128)(2,1)}, u32[]{:S(2)}) copy-start(bf16[256,16,8]{0,2,1:T(8,128)(2,1)} %get-tuple-element.110) | copy-start | bytes 196612
  145.0 75.6 %copy-start.23 = (bf16[256,16,8]{0,2,1:T(8,128)(2,1)S(1)}, bf16[256,16,8]{0,2,1:T(8,128)(2,1)}, u32[]{:S(2)}) copy-start(bf16[256,16,8]{0,2,1:T(8,128)(2,1)} %get-tuple-element.111) | copy-start | bytes 196612
  145.0 421.6 %all-gather.20.cloned.1.call-start = ((), (), s32[]{:S(2)}) async-start(), calls=%async_computation.9 | async-start | bytes 10485760 | tf_op jit(solution)/shard_map/all_gather | solution.py:144
  145.6 498.3 %reduce-scatter.7.cloned.1.call-start = ((), (), s32[]{:S(2)}) async-start(), calls=%async_computation.11 | async-start | bytes 5242880 | tf_op jit(solution)/shard_map/reduce_scatter | solution.py:216
  177.3 47.9 %copy-start.12 = (bf16[256,16,48]{0,2,1:T(8,128)(2,1)}, bf16[256,16,48]{0,2,1:T(8,128)(2,1)S(1)}, u32[]{:S(2)}) copy-start(bf16[256,16,48]{0,2,1:T(8,128)(2,1)S(1)} %fusion.83) | copy-start | bytes 1179652
  267.2 15.4 slice-start
  267.2 15.4 slice-start.1
  267.2 16.4 slice-start.2
  267.2 17.6 slice-start.3
  299.4 424.2 %reduce-scatter.9.cloned.1.call-start = ((), (), s32[]{:S(2)}) async-start(), calls=%async_computation.12 | async-start | bytes 5242880 | tf_op jit(solution)/shard_map/reduce_scatter | solution.py:217
  309.6 493.6 %reduce-scatter.13.cloned.1.call-start = ((), (), s32[]{:S(2)}) async-start(), calls=%async_computation.14 | async-start | bytes 5242880 | tf_op jit(solution)/shard_map/reduce_scatter | solution.py:195
  322.2 15.1 copy-start.41
  322.2 23.9 %copy-start.42 = (bf16[256]{0:T(256)(128)(2,1)S(1)}, bf16[256]{0:T(256)(128)(2,1)}, u32[]{:S(2)}) copy-start(bf16[256]{0:T(256)(128)(2,1)} %param.19) | copy-start | bytes 1540
  322.3 764.1 %reduce-scatter.15.cloned.1.call-start = ((), (), s32[]{:S(2)}) async-start(), calls=%async_computation.15 | async-start | bytes 20971520 | tf_op jit(solution)/shard_map/reduce_scatter | solution.py:255
  357.5 209.2 %copy-start.2 = (bf16[1,256,1024]{2,1,0:T(8,128)(2,1)S(1)}, bf16[1,256,1024]{2,1,0:T(8,128)(2,1)}, u32[]{:S(2)}) copy-start(bf16[1,256,1024]{2,1,0:T(8,128)(2,1)} %param.14) | copy-start | bytes 1572868
  357.5 209.2 %copy-start.33 = (f32[256]{0:T(256)S(1)}, f32[256]{0:T(256)}, u32[]{:S(2)}) copy-start(f32[256]{0:T(256)} %copy-done.32) | copy-start | bytes 3076
  566.6 15.9 copy-start.3
  582.5 17.5 copy-start.15
  599.7 770.1 %reduce-scatter.17.cloned.1.call-start = ((), (), s32[]{:S(2)}) async-start(), calls=%async_computation.16 | async-start | bytes 20971520 | tf_op jit(solution)/shard_map/reduce_scatter | solution.py:196
  608.2 976.6 %reduce-scatter.11.cloned.1.call-start = ((), (), s32[]{:S(2)}) async-start(), calls=%async_computation.13 | async-start | bytes 15728640 | tf_op jit(solution)/shard_map/reduce_scatter | solution.py:253
  616.7 29.7 %slice-start.4 = ((f32[1,256,16,64]{1,3,2,0:T(8,128)}), f32[1,256,16,48]{1,3,2,0:T(8,128)S(1)}, s32[]{:S(2)}) async-start(f32[1,256,16,64]{1,3,2,0:T(8,128)} %copy-done.9), calls=%async_computation.23 | async-start | bytes 1572864 | tf_op jit(solution)/shard_map/transpose(jvp())/split | solution.py:42
  733.2 1030.8 %all-reduce.18.cloned.1.call-start = ((), (), s32[]{:S(2)}) async-start(), calls=%async_computation.18 | async-start | bytes 25165824 | tf_op jit(solution)/shard_map/psum | solution.py:258
  (31 other events, 131.0 us)
Sparse Core Ops, SparseCore 0:
  9.6 118.1 all-gather.13
  129.4 44.1 all-gather.17
  175.7 44.9 all-gather.15
  222.6 44.4 all-gather.23
  269.1 148.0 all-gather.21
  418.7 147.8 all-gather.19
  568.9 74.9 reduce-scatter.6
  646.3 77.2 reduce-scatter.8
  725.9 77.2 reduce-scatter.12
  805.6 280.7 reduce-scatter.14
  1088.8 281.0 reduce-scatter.16
  1372.2 212.5 reduce-scatter.10
  1589.3 174.6 all-reduce.17
where the time goes:
time: 1790 us; the launch traced here: 1780 us
  waiting for transfers between devices  1440 us (80%)
  matrix products  126 us (7%)
  blocking collectives  120 us (7%)
  local copies, waits for them, and re-layouts  55.4 us (3%)
  other arithmetic  26.3 us (1%)
    reduce_scatter x1, waiting for transfers between devices, shards(): lax.psum_scatter(grad_down_weight, 'shard', scatter_dimension=0, tiled=True)  283 us
    reduce_scatter x1, waiting for transfers between devices, shards(): lax.psum_scatter(grad_up_weight, 'shard', scatter_dimension=0, tiled=True)  283 us
    reduce_scatter x1, waiting for transfers between devices, shards(): lax.psum_scatter(grad_qkv_weight, 'shard', scatter_dimension=0, tiled=True)  215 us
    all_gather x1, waiting for transfers between devices, shards(): lax.all_gather(up_weight, 'shard', axis=0, tiled=True)  135 us
    psum x1, waiting for transfers between devices, shards(): lax.psum((in_shares[0], in_shares[1], in_shares[2], in_shares[3], in_shar...  101 us
    all_gather x1, waiting for transfers between devices, shards(): lax.all_gather(qkv_weight, 'shard', axis=0, tiled=True)  77.4 us
    reduce_scatter x1, waiting for transfers between devices, shards(): lax.psum_scatter(value_part, 'shard', scatter_dimension=1, tiled=True)  76.4 us
    reduce_scatter x1, waiting for transfers between devices, shards(): lax.psum_scatter(grad_out_weight, 'shard', scatter_dimension=0, tiled=True)  70 us
  transfers between devices with their start and end apart: 13, of which 13 were waited for; matrix products, arithmetic and copies ran while one was open for 10% of the time, Pallas kernels for 0%

commit v1 on v0

--- a/solution.py
+++ b/solution.py
@@ -10,6 +10,28 @@
 HEAD = 64
 ROT = 16
 DOCS = 3
+
+
+def in_order(blocks, dim):
+    blocks = jnp.moveaxis(blocks, 0, dim)
+    shape = blocks.shape
+    return blocks.reshape(*shape[:dim], shape[dim] * shape[dim + 1], *shape[dim + 2 :])
+
+
+def ring_gather(x, axis, dim):
+    size = lax.axis_size(axis)
+    pairs = [(i, (i + 1) % size) for i in range(size)]
+    back = [(b, a) for a, b in pairs]
+    lower, upper = ([], [])
+    for hop in range(size - 1):
+        if hop % 2 == 0:
+            lower.append(lax.ppermute(lower[-1] if lower else x, axis, pairs))
+        else:
+            upper.append(lax.ppermute(upper[-1] if upper else x, axis, back))
+    pieces = jnp.stack([*lower[::-1], x, *upper])
+    shift = lax.axis_index(axis) - len(lower)
+    pieces = pieces[(jnp.arange(size) - shift) % size]
+    return in_order(pieces, dim)
 
 
 def layer_norm(values, gain, shift):
@@ -173,7 +195,7 @@
     down_grouped = down_weight.reshape(-1, group_ratio * model_width)
     pieces = (
         lax.all_gather(out_weight, "shard", axis=0, tiled=True),
-        lax.all_gather(down_grouped, "shard", axis=0, tiled=True),
+        ring_gather(down_grouped, "shard", 0),
     )
     piece_rows = pieces[0].shape[0]
     down_rows = pieces[1].reshape(piece_rows * group_ratio, model_width)

time: 1790 us -> 1910 us (1.067)
  blocking collectives: 120 us -> 261 us
  waiting for transfers between devices: 1440 us -> 1370 us
  local copies, waits for them, and re-layouts: 55.4 us -> 88 us
    all_gather x1, blocking collectives: 10.9 us -> 148 us  [shards(): lax.all_gather(output_bias, 'shard', axis=0, tiled=True)]
    ppermute x0 -> x3, waiting for transfers between devices: none -> 91.7 us  [the longest x2 91.7 us: ring_gather(): lower.append(lax.ppermute(lower[-1] if lower else x, axis, pairs))]
    reduce_scatter x1, waiting for transfers between devices: 70 us -> 0.02 us  [shards(): lax.psum_scatter(grad_out_weight, 'shard', scatter_dimension=0, tiled=True)]
    reduce_scatter x1, waiting for transfers between devices: 283 us -> 227 us  [shards(): lax.psum_scatter(grad_up_weight, 'shard', scatter_dimension=0, tiled=True)]
    psum x1, waiting for transfers between devices: 101 us -> 70.9 us  [shards(): lax.psum((in_shares[0], in_shares[1], in_shares[2], in_shares[3], in_shar...]
  transfers between devices with their start and end apart: 13 -> 16, of which waited for: 13 -> 13; matrix products, arithmetic and copies ran while one was open for 10% -> 12% of each run, Pallas kernels for 0% -> 0%
where the time goes in v1:
time: 1910 us; the launch traced here: 1900 us
  waiting for transfers between devices  1370 us (72%)
  blocking collectives  261 us (14%)
  matrix products  127 us (7%)
  local copies, waits for them, and re-layouts  88 us (5%)
  other arithmetic  37.3 us (2%)
    reduce_scatter x1, waiting for transfers between devices, shards(): lax.psum_scatter(grad_down_weight, 'shard', scatter_dimension=0, tiled=True)  283 us
    reduce_scatter x1, waiting for transfers between devices, shards(): lax.psum_scatter(grad_up_weight, 'shard', scatter_dimension=0, tiled=True)  227 us
    reduce_scatter x1, waiting for transfers between devices, shards(): lax.psum_scatter(grad_qkv_weight, 'shard', scatter_dimension=0, tiled=True)  215 us
    all_gather x1, blocking collectives, shards(): lax.all_gather(output_bias, 'shard', axis=0, tiled=True)  148 us
    all_gather x1, waiting for transfers between devices, shards(): lax.all_gather(up_weight, 'shard', axis=0, tiled=True)  135 us
    ppermute x2, waiting for transfers between devices, ring_gather(): lower.append(lax.ppermute(lower[-1] if lower else x, axis, pairs))  91.7 us
    reduce_scatter x1, waiting for transfers between devices, shards(): lax.psum_scatter(value_part, 'shard', scatter_dimension=1, tiled=True)  78.2 us
    all_gather x1, waiting for transfers between devices, shards(): lax.all_gather(qkv_weight, 'shard', axis=0, tiled=True)  77.3 us
  transfers between devices with their start and end apart: 16, of which 13 were waited for; matrix products, arithmetic and copies ran while one was open for 12% of the time, Pallas kernels for 0%

profile of v1, /device:TPU:0, one launch (start us, length us, event | category | flops | bytes accessed | tf_op | source)
XLA Modules:
  0.0 1903.6 jit_solution(11055341235827318222)
XLA Ops:
  9.4 12.6 all-gather.1
  22.6 7.7 all-gather.2
  31.1 13.7 all-gather.3
  50.6 77.3 %all-gather.14.cloned.1.call-done = bf16[1024,3072]{1,0:T(8,128)(2,1)} async-done(((bf16[256,3072]{1,0:T(8,128)(2,1)}), bf16[1024,3072]{1,0:T(8,128)(2,1)}) %all-gather.14.cloned.1.call-update) | async-done | bytes 6291472 | tf_op jit(solution)/shard_map/all_gather | solution.py:165
  146.6 27.1 %all-gather.18.cloned.1.call-done = bf16[1024,1024]{1,0:T(8,128)(2,1)} async-done(((bf16[256,1024]{1,0:T(8,128)(2,1)}), bf16[1024,1024]{1,0:T(8,128)(2,1)}) %all-gather.18.cloned.1.call-update) | async-done | bytes 2097168 | tf_op jit(solution)/shard_map/all_gather | solution.py:197
  177.5 43.3 %all-gather.16.cloned.1.call-done = bf16[1,1024,16,64]{1,3,2,0:T(8,128)(2,1)} async-done(((bf16[1,256,16,64]{1,3,2,0:T(8,128)(2,1)}), bf16[1,1024,16,64]{1,3,2,0:T(8,128)(2,1)}) %all-gather.16.cloned.1.call-update) | async-done | bytes 2097168 | tf_op jit(solution)/shard_map/all_gather | solution.py:186
  232.1 35.2 %all-gather.24.cloned.1.call-done = bf16[1,1024,1,16,64]{1,4,3,2,0:T(8,128)(2,1)} async-done(((bf16[1,256,1,16,64]{1,4,3,2,0:T(8,128)(2,1)}), bf16[1,1024,1,16,64]{1,4,3,2,0:T(8,128)(2,1)}) %all-gather.24.cloned.1.call-update) | async-done | bytes 2097168 | tf_op jit(solution)/shard_map/all_gather | solution.py:187
  267.3 15.4 multiply_reduce_fusion
  285.1 7.8 multiply_convert_fusion
  300.5 9.5 fusion.12
  323.3 8.2 all-gather.4
  331.5 13.9 all-gather.5
  345.5 14.9 all_gather.52
  360.3 56.5 %all-gather.22.cloned.1.call-done = bf16[1024,4096]{1,0:T(8,128)(2,1)} async-done(((bf16[256,4096]{1,0:T(8,128)(2,1)}), bf16[1024,4096]{1,0:T(8,128)(2,1)}) %all-gather.22.cloned.1.call-update) | async-done | bytes 8388624 | tf_op jit(solution)/shard_map/all_gather | solution.py:224
  416.9 14.3 reshape.617
  431.2 135.1 %all-gather.20.cloned.1.call-done = bf16[1024,4096]{1,0:T(8,128)(2,1)} async-done(((bf16[256,4096]{1,0:T(8,128)(2,1)}), bf16[1024,4096]{1,0:T(8,128)(2,1)}) %all-gather.20.cloned.1.call-update) | async-done | bytes 8388624 | tf_op jit(solution)/shard_map/all_gather | solution.py:166
  566.2 15.8 multiply_convert_fusion.1
  591.1 8.3 fusion.94
  599.7 8.1 fusion.66
  616.4 27.1 %reduce-scatter.7.cloned.1.call-done = f32[1,256,16,64]{1,3,2,0:T(8,128)} async-done(((f32[1,1024,16,64]{1,3,2,0:T(8,128)}), f32[1,256,16,64]{1,3,2,0:T(8,128)}) %reduce-scatter.7.cloned.1.call-update) | async-done | bytes 1048592 | tf_op jit(solution)/shard_map/reduce_scatter | solution.py:238
  645.0 78.2 %reduce-scatter.9.cloned.1.call-done = f32[1,256,16,64]{1,3,2,0:T(8,128)} async-done(((f32[1,1024,16,64]{1,3,2,0:T(8,128)}), f32[1,256,16,64]{1,3,2,0:T(8,128)}) %reduce-scatter.9.cloned.1.call-update) | async-done | bytes 1048592 | tf_op jit(solution)/shard_map/reduce_scatter | solution.py:239
  726.1 7.7 fusion.62
  737.8 91.7 %collective-permute-done = bf16[256,4096]{1,0:T(8,128)(2,1)} collective-permute-done((bf16[256,4096]{1,0:T(8,128)(2,1)}, bf16[256,4096]{1,0:T(8,128)(2,1)}, u32[]{:S(2)}, u32[]{:S(2)}) %collective-permute-start) | collective-permute-done | bytes 2097184 | tf_op jit(solution)/shard_map/ppermute | solution.py:28
  834.6 147.6 %all-gather.6 = bf16[4,1,256]{2,1,0:T(2,128)(2,1)S(1)} all-gather(bf16[1,1,256]{2,1,0:T(2,128)(2,1)S(1)} %reshape.647), channel_id=1, replica_groups=mesh['replica'=8,'shard'=4] {'shard'}, dimensions={0}, use_global_device_ids=true | all-gather | bytes 2560 | tf_op jit(solution)/shard_map/all_gather | solution.py:154
  982.2 227.0 %reduce-scatter.15.cloned.1.call-done = f32[256,4096]{1,0:T(8,128)} async-done(((f32[1024,4096]{1,0:T(8,128)}), f32[256,4096]{1,0:T(8,128)}) %reduce-scatter.15.cloned.1.call-update) | async-done | bytes 4194320 | tf_op jit(solution)/shard_map/reduce_scatter | solution.py:277
  1209.2 282.8 %reduce-scatter.17.cloned.1.call-done = f32[1024,1024]{1,0:T(8,128)} async-done(((f32[4096,1024]{1,0:T(8,128)}), f32[1024,1024]{1,0:T(8,128)}) %reduce-scatter.17.cloned.1.call-update) | async-done | bytes 4194320 | tf_op jit(solution)/shard_map/reduce_scatter | solution.py:218
  1492.0 214.9 %reduce-scatter.11.cloned.1.call-done = f32[256,3072]{1,0:T(8,128)} async-done(((f32[1024,3072]{1,0:T(8,128)}), f32[256,3072]{1,0:T(8,128)}) %reduce-scatter.11.cloned.1.call-update) | async-done | bytes 3145744 | tf_op jit(solution)/shard_map/reduce_scatter | solution.py:275
  1726.8 8.0 pad_maximum_fusion.1
  1734.8 14.4 reshape_reshape.3
  1772.6 18.9 all-reduce.15
  1791.9 23.3 %all-reduce.13 = (f32[256]{0:T(256)}, f32[256]{0:T(256)}, f32[256]{0:T(256)}, f32[256]{0:T(256)}, f32[768]{0:T(1024)}, /*index=5*/f32[1024]{0:T(1024)}, f32[256]{0:T(256)}) all-reduce(f32[256]{0:T(256)S(1)} %dynamic-slice.3, f32[256]{0:T(256)S(1)} %dynamic-slice.5, ...), channel_id=1, replica_groups=mesh['replica'=8,'shard'=4] {'replica'}, use_global_device_ids=true, to_apply=%region_16.17 | all-reduce | flops 3072 | bytes 24576 | tf_op jit(solution)/shard_map/psum | solution.py:280
  1815.2 70.9 %all-reduce.18.cloned.1.call-done = (f32[256,3072]{1,0:T(8,128)}, f32[256,1024]{1,0:T(8,128)}, f32[256,4096]{1,0:T(8,128)}, f32[1024,1024]{1,0:T(8,128)}) async-done(((f32[256,3072]{1,0:T(8,128)}, f32[256,1024]{1,0:T(8,128)}, f32[256,4096]{1,0:T(8,128)}, f32[1024,1024]{1,0:T(8,128)}), (f32[256,3072]{1,0:T(8,128)}, f32[256,1024]{1,0:T(8,128)}, f32[256,4096]{1,0:T(8,128)}, ...) | async-done | bytes 12582928 | tf_op jit(solution)/shard_map/psum | solution.py:280
  (221 shorter events, 149.7 us)
Async XLA Ops:
  7.2 120.7 %all-gather.14.cloned.1.call-start = ((), (), s32[]{:S(2)}) async-start(), calls=%async_computation.6 | async-start | bytes 7864320 | tf_op jit(solution)/shard_map/all_gather | solution.py:165
  7.9 165.8 %all-gather.18.cloned.1.call-start = ((), (), s32[]{:S(2)}) async-start(), calls=%async_computation.8 | async-start | bytes 2621440 | tf_op jit(solution)/shard_map/all_gather | solution.py:197
  8.7 212.1 %all-gather.16.cloned.1.call-start = ((), (), s32[]{:S(2)}) async-start(), calls=%async_computation.7 | async-start | bytes 2621440 | tf_op jit(solution)/shard_map/all_gather | solution.py:186
  50.4 84.0 %copy-start.41 = (f32[256]{0:T(256)}, f32[256]{0:T(256)S(1)}, u32[]{:S(2)}) copy-start(f32[256]{0:T(256)S(1)} %fusion.53) | copy-start | bytes 3076
  50.5 84.0 %copy-start.36 = (f32[256]{0:T(256)}, f32[256]{0:T(256)S(1)}, u32[]{:S(2)}) copy-start(f32[256]{0:T(256)S(1)} %fusion.89) | copy-start | bytes 3076
  50.6 86.6 %copy-start.32 = (f32[256,8]{0,1:T(8,128)}, f32[256,8]{0,1:T(8,128)S(1)}, u32[]{:S(2)}) copy-start(f32[256,8]{0,1:T(8,128)S(1)} %get-tuple-element.124) | copy-start | bytes 24580
  50.6 86.6 %copy-start.33 = (f32[256,8]{0,1:T(8,128)}, f32[256,8]{0,1:T(8,128)S(1)}, u32[]{:S(2)}) copy-start(f32[256,8]{0,1:T(8,128)S(1)} %get-tuple-element.125) | copy-start | bytes 24580
  139.7 127.6 %all-gather.24.cloned.1.call-start = ((), (), s32[]{:S(2)}) async-start(), calls=%async_computation.17 | async-start | bytes 2621440 | tf_op jit(solution)/shard_map/all_gather | solution.py:187
  140.6 33.0 %copy-start.9 = (bf16[1,256,1024]{2,1,0:T(8,128)(2,1)S(1)}, bf16[1,256,1024]{2,1,0:T(8,128)(2,1)}, u32[]{:S(2)}) copy-start(bf16[1,256,1024]{2,1,0:T(8,128)(2,1)} %param.15) | copy-start | bytes 1572868
  140.6 276.2 %all-gather.22.cloned.1.call-start = ((), (), s32[]{:S(2)}) async-start(), calls=%async_computation.12 | async-start | bytes 10485760 | tf_op jit(solution)/shard_map/all_gather | solution.py:224
  145.2 75.6 %copy-start.25 = (bf16[256,16,8]{0,2,1:T(8,128)(2,1)S(1)}, bf16[256,16,8]{0,2,1:T(8,128)(2,1)}, u32[]{:S(2)}) copy-start(bf16[256,16,8]{0,2,1:T(8,128)(2,1)} %get-tuple-element.112) | copy-start | bytes 196612
  145.2 75.6 %copy-start.27 = (bf16[256,16,8]{0,2,1:T(8,128)(2,1)S(1)}, bf16[256,16,8]{0,2,1:T(8,128)(2,1)}, u32[]{:S(2)}) copy-start(bf16[256,16,8]{0,2,1:T(8,128)(2,1)} %get-tuple-element.113) | copy-start | bytes 196612
  145.2 421.0 %all-gather.20.cloned.1.call-start = ((), (), s32[]{:S(2)}) async-start(), calls=%async_computation.9 | async-start | bytes 10485760 | tf_op jit(solution)/shard_map/all_gather | solution.py:166
  145.8 497.8 %reduce-scatter.7.cloned.1.call-start = ((), (), s32[]{:S(2)}) async-start(), calls=%async_computation.10 | async-start | bytes 5242880 | tf_op jit(solution)/shard_map/reduce_scatter | solution.py:238
  177.5 47.9 %copy-start.16 = (bf16[256,16,48]{0,2,1:T(8,128)(2,1)}, bf16[256,16,48]{0,2,1:T(8,128)(2,1)S(1)}, u32[]{:S(2)}) copy-start(bf16[256,16,48]{0,2,1:T(8,128)(2,1)S(1)} %fusion.83) | copy-start | bytes 1179652
  267.3 17.7 slice-start.3
  299.8 423.4 %reduce-scatter.9.cloned.1.call-start = ((), (), s32[]{:S(2)}) async-start(), calls=%async_computation.11 | async-start | bytes 5242880 | tf_op jit(solution)/shard_map/reduce_scatter | solution.py:239
  310.0 672.2 %reduce-scatter.13.cloned.1.call-start = ((), (), s32[]{:S(2)}) async-start(), calls=%async_computation.14 | async-start | bytes 5242880 | tf_op jit(solution)/shard_map/reduce_scatter | solution.py:217
  322.7 22.8 %copy-start.44 = (bf16[1024]{0:T(1024)(128)(2,1)S(1)}, bf16[1024]{0:T(1024)(128)(2,1)}, u32[]{:S(2)}) copy-start(bf16[1024]{0:T(1024)(128)(2,1)} %param.25) | copy-start | bytes 6148
  322.7 886.5 %reduce-scatter.15.cloned.1.call-start = ((), (), s32[]{:S(2)}) async-start(), calls=%async_computation.15 | async-start | bytes 20971520 | tf_op jit(solution)/shard_map/reduce_scatter | solution.py:277
  360.3 205.9 %copy-start.2 = (bf16[1,256,1024]{2,1,0:T(8,128)(2,1)S(1)}, bf16[1,256,1024]{2,1,0:T(8,128)(2,1)}, u32[]{:S(2)}) copy-start(bf16[1,256,1024]{2,1,0:T(8,128)(2,1)} %param.14) | copy-start | bytes 1572868
  360.3 205.9 %copy-start.37 = (f32[256]{0:T(256)S(1)}, f32[256]{0:T(256)}, u32[]{:S(2)}) copy-start(f32[256]{0:T(256)} %copy-done.36) | copy-start | bytes 3076
  582.1 17.6 copy-start.19
  599.4 892.6 %reduce-scatter.17.cloned.1.call-start = ((), (), s32[]{:S(2)}) async-start(), calls=%async_computation.16 | async-start | bytes 20971520 | tf_op jit(solution)/shard_map/reduce_scatter | solution.py:218
  607.8 1099.1 %reduce-scatter.11.cloned.1.call-start = ((), (), s32[]{:S(2)}) async-start(), calls=%async_computation.13 | async-start | bytes 15728640 | tf_op jit(solution)/shard_map/reduce_scatter | solution.py:275
  733.8 95.7 %copy-start.4 = (bf16[1024,1024]{1,0:T(8,128)(2,1)S(1)}, bf16[1024,1024]{1,0:T(8,128)(2,1)}, u32[]{:S(2)}) copy-start(bf16[1024,1024]{1,0:T(8,128)(2,1)} %param.26) | copy-start | bytes 6291460
  733.8 98.2 %copy-start.48 = (u32[32]{0:T(128)S(1)}, u32[32]{0:T(128)}, u32[]{:S(2)}) copy-start(u32[32]{0:T(128)} %constant.193) | copy-start | bytes 388
  733.9 100.7 %copy-start.47 = (bf16[256]{0:T(256)(128)(2,1)S(1)}, bf16[256]{0:T(256)(128)(2,1)}, u32[]{:S(2)}) copy-start(bf16[256]{0:T(256)(128)(2,1)} %param.27) | copy-start | bytes 1540
  733.9 1152.2 %all-reduce.18.cloned.1.call-start = ((), (), s32[]{:S(2)}) async-start(), calls=%async_computation.18 | async-start | bytes 25165824 | tf_op jit(solution)/shard_map/psum | solution.py:280
  733.9 95.6 %collective-permute-start = (bf16[256,4096]{1,0:T(8,128)(2,1)}, bf16[256,4096]{1,0:T(8,128)(2,1)}, u32[]{:S(2)}, u32[]{:S(2)}) collective-permute-start(bf16[256,4096]{1,0:T(8,128)(2,1)} %reshape.614), channel_id=1, source_target_pairs={{0,1},{1,2},{2,3},{3,0},{4,5},{5,6},{6,7},{7,4},{8,9},{9,10},{10,1... | collective-permute-start | bytes 6291464 | tf_op jit(solution)/shard_map/ppermute | solution.py:28
  735.4 971.5 %collective-permute-start.2 = (bf16[256,4096]{1,0:T(8,128)(2,1)}, bf16[256,4096]{1,0:T(8,128)(2,1)}, u32[]{:S(2)}, u32[]{:S(2)}) collective-permute-start(bf16[256,4096]{1,0:T(8,128)(2,1)} %reshape.614), channel_id=1, source_target_pairs={{1,0},{2,1},{3,2},{0,3},{5,4},{6,5},{7,6},{4,7},{9,8},{10,9},{11,1... | collective-permute-start | bytes 6291464 | tf_op jit(solution)/shard_map/ppermute | solution.py:30
  829.5 877.5 %collective-permute-start.1 = (bf16[256,4096]{1,0:T(8,128)(2,1)}, bf16[256,4096]{1,0:T(8,128)(2,1)}, u32[]{:S(2)}, u32[]{:S(2)}) collective-permute-start(bf16[256,4096]{1,0:T(8,128)(2,1)} %collective-permute-done), channel_id=1, source_target_pairs={{0,1},{1,2},{2,3},{3,0},{4,5},{5,6},{6,7},{7,4},{8,9},{9,10},{10,1... | collective-permute-start | bytes 6291464 | tf_op jit(solution)/shard_map/ppermute | solution.py:28
  (38 other events, 202.7 us)
Sparse Core Ops, SparseCore 0:
  9.6 118.2 all-gather.13
  129.4 44.1 all-gather.17
  175.8 44.9 all-gather.15
  222.8 44.4 all-gather.23
  268.7 148.0 all-gather.21
  418.3 147.8 all-gather.19
  568.5 74.9 reduce-scatter.6
  645.9 77.2 reduce-scatter.8
  725.5 154.1 reduce-scatter.12
  882.0 327.1 reduce-scatter.14
  1211.6 280.3 reduce-scatter.16
  1494.3 212.5 reduce-scatter.10
  1711.4 174.6 all-reduce.17
